TPU v7x, 768 devices: a whole 4x8x12 slice. The times are simulated.
768 devices in a mesh: tile: 48 (over z_lo, y, core), layer: 16 (over z_hi, x).
Axes of the slice: x: 4, y: 8, z: 12 (z_hi: 4, z_lo: 3; z = z_hi * 3 + z_lo), core: 2. Of those that a mesh axis runs over, the one named last changes fastest.
Arguments:
- adjoint: float32 [32, 2, 384, 2048], P('layer', None, 'tile'), may hold values from -6 to 6
- source: float32 [32, 2, 384, 2048], P('layer', None, 'tile'), may hold values from -6 to 6
- viscosity: float32 [32, 384, 2048], P('layer', 'tile'), may hold values from 0.3 to 3
- vertical: float32 [32, 384, 2048], P(None, 'tile', 'layer'), may hold values from 1 to 30
- friction: float32 [384, 2048], P('tile', 'layer'), may hold values from 0.1 to 10
- ice_mask: int32 [384, 2048], P('tile', 'layer'), may hold values 0 or 1
- gate_cells: int32 [1536, 64], P('layer'), may hold values from 0 to 786431
- gate_owner: int32 [1536], replicated, may hold values from 0 to 767, as said below
Outputs:
- adjoint_new: float32 [32, 2, 384, 2048], P('layer', None, 'tile')
- gate_flux: float32 [768, 2], P(('tile', 'layer'))
Inputs may be any that keep to these rules, and one draw needn't show every extreme that they name: `gate_owner`: every owner id appears exactly 2 times.
All inputs are finite; a program needn't handle non-finite values. No bound on the sum of `ice_mask` on one device may be relied on, other than what follows from the above.
Results may differ from a plain program's by a relative error of at most 0.000028.
Values sent between devices are 32-bit elements; how exact they have to be, the bound alone decides.
A program may use at most 32 MiB of HBM per device.

v0:
```python
import jax
import jax.numpy as jnp
from jax import lax
from jax.sharding import PartitionSpec as P

SLOTS = 2


step_scale = 0.2


def extended(block, sides, width):
    for axis, dim in sides:
        count = lax.axis_size(axis)
        forward = [(i, i + 1) for i in range(count - 1)]
        backward = [(target, source) for source, target in forward]
        low = lax.ppermute(
            lax.slice_in_dim(block, block.shape[dim] - width, None, axis=dim), axis, forward
        )
        high = lax.ppermute(lax.slice_in_dim(block, 0, width, axis=dim), axis, backward)
        block = jnp.concatenate([low, block, high], axis=dim)
    return block


def stencil(padded, viscosity):
    centre = padded[:, :, 1:-1, 1:-1]
    beside = (
        padded[:, :, 2:, 1:-1]
        + padded[:, :, :-2, 1:-1]
        + padded[:, :, 1:-1, 2:]
        + padded[:, :, 1:-1, :-2]
    )
    cross_term = 0.25 * (
        padded[:, :, 2:, 2:]
        - padded[:, :, 2:, :-2]
        - padded[:, :, :-2, 2:]
        + padded[:, :, :-2, :-2]
    )
    return viscosity[:, None] * (beside - 4.0 * centre + cross_term[:, ::-1])


def column_solve(rhs, vertical, friction):
    zero_plane = jnp.zeros_like(friction)

    def forward(state, layer_terms):
        below_prev, link_prev, ratio_prev, scaled_prev = state
        vert_k, rhs_k = layer_terms
        diag_k = 1.0 + below_prev + vert_k
        pivot_value = diag_k - link_prev * ratio_prev
        ratio_new = vert_k / pivot_value
        scaled_new = (rhs_k + link_prev[None] * scaled_prev) / pivot_value[None]
        return ((vert_k, vert_k, ratio_new, scaled_new), (ratio_new, scaled_new))

    initial = (friction, zero_plane, zero_plane, jnp.zeros_like(rhs[0]))
    _, (ratios, scaled) = lax.scan(forward, initial, (vertical, rhs))

    def backward(upper_value, layer_terms):
        ratio_k, scaled_k = layer_terms
        solved_value = scaled_k + ratio_k[None] * upper_value
        return (solved_value, solved_value)

    _, solved = lax.scan(backward, jnp.zeros_like(rhs[0]), (ratios, scaled), reverse=True)
    return solved


def owner_order(gate_owner):
    return jnp.argsort(gate_owner, stable=True)


def local(adjoint, source, viscosity, vertical, friction, ice_mask, gate_cells, gate_owner):
    with_rims = extended(adjoint, (("tile", 2),), 1)
    padded = jnp.pad(with_rims, ((0, 0), (0, 0), (0, 0), (1, 1)))
    rhs = source + step_scale * stencil(padded, viscosity)
    active = ice_mask.astype(jnp.float32)[None, None]
    gathered = lax.all_to_all(rhs, "layer", split_axis=3, concat_axis=0, tiled=True)
    columns = column_solve(gathered, vertical, friction) * active
    updated = lax.all_to_all(columns, "layer", split_axis=0, concat_axis=3, tiled=True)
    layer_total = columns.shape[0]
    tile_rows = columns.shape[2]
    tile_count = lax.axis_size("tile")
    layer_count = lax.axis_size("layer")
    discharge = jnp.sum(columns, axis=(0, 1)) / layer_total
    tile_table = lax.all_gather(discharge, "layer", axis=1, tiled=True)
    map_width = tile_table.shape[1]
    first_row = lax.axis_index("tile") * tile_rows
    cell_row = gate_cells // map_width
    cell_col = gate_cells % map_width
    inside = (cell_row >= first_row) & (cell_row < first_row + tile_rows)
    local_index = jnp.clip(
        (cell_row - first_row) * map_width + cell_col, 0, tile_rows * map_width - 1
    )
    picked = jnp.where(inside, tile_table.reshape(-1)[local_index], 0.0)
    partial_value = jnp.sum(picked, axis=1)
    gate_count = gate_owner.shape[0]
    whole_list = lax.dynamic_update_slice_in_dim(
        jnp.zeros((gate_count,), jnp.float32),
        partial_value,
        lax.axis_index("layer") * partial_value.shape[0],
        0,
    )
    owner_table = whole_list[owner_order(gate_owner)]
    gate_flux = lax.psum_scatter(
        owner_table.reshape(tile_count * layer_count, SLOTS),
        ("tile", "layer"),
        scatter_dimension=0,
        tiled=True,
    )
    return (updated, gate_flux)


def solution(mesh):
    placed = (
        P("layer", None, "tile", None),
        P("layer", None, "tile", None),
        P("layer", "tile", None),
        P(None, "tile", "layer"),
        P("tile", "layer"),
        P("tile", "layer"),
        P("layer", None),
        P(),
    )
    return jax.shard_map(
        local,
        mesh=mesh,
        in_specs=placed,
        out_specs=(P("layer", None, "tile", None), P(("tile", "layer"), None)),
        check_vma=False,
    )
```

profile of v0, /device:TPU:1, one launch (start us, length us, event | category | flops | bytes accessed | tf_op | source)
XLA Modules:
  0.0 308.9 jit_solution(17009510852049920193)
XLA Ops:
  0.6 1.1 fusion.16
  1.8 12.4 %collective-permute-start = (f32[2,2,1,2048]{3,1,2,0:T(2,128)S(1)}, f32[2,2,1,2048]{3,1,2,0:T(2,128)S(1)}, u32[]{:S(2)}, u32[]{:S(2)}) collective-permute-start(f32[2,2,1,2048]{3,1,2,0:T(2,128)S(1)} %copy.94), channel_id=1, source_target_pairs={{16,0},{32,16},{48,32},{64,48},{80,64},{96,80},{112,96},{128,112},... | collective-permute-start | bytes 98312 | tf_op jit(solution)/shard_map/ppermute | solution.py:20
  14.2 1.9 collective-permute-start.1
  16.2 1.1 collective-permute-done.1
  17.4 1.3 select_maximum_fusion
  18.9 1.6 fusion.7
  20.6 4.3 %copy.87 = f32[2,2,8,2048]{2,1,0,3:T(2,128)} copy(f32[2,2,8,2048]{3,2,1,0:T(8,128)S(1)} %fusion.7) | data formatting | bytes 524288 | tf_op jit(solution)/shard_map/add | solution.py:73
  24.9 8.9 %reshape.35 = f32[16,1,4096]{2,1,0:T(1,128)} reshape(f32[2048,2,2,8]{3,2,1,0:T(2,128)} %bitcast.42) | data formatting | bytes 524288
  33.8 8.8 %all-to-all-start = ((f32[16,1,4096]{2,1,0:T(1,128)}), f32[16,1,4096]{2,1,0:T(1,128)S(1)}, u32[]{:S(2)}, u32[]{:S(2)}) async-start(f32[16,1,4096]{2,1,0:T(1,128)} %reshape.35), calls=%async_computation | async-start | bytes 524288 | tf_op jit(solution)/shard_map/all_to_all | solution.py:75
  42.8 5.0 %sort.17 = (s32[1536]{0:T(1024)}, s32[1536]{0:T(1024)S(1)}) sort(s32[1536]{0:T(1024)S(1)} %copy-done.2, s32[1536]{0:T(1024)S(1)} %iota.4), dimensions={0}, to_apply=%region_6.7 | sort | flops 16896 | bytes 24576 | tf_op jit(solution)/shard_map/jit(argsort)/sort | solution.py:67
  47.9 7.9 %all-to-all-done = f32[16,1,4096]{2,1,0:T(1,128)S(1)} async-done(((f32[16,1,4096]{2,1,0:T(1,128)}), f32[16,1,4096]{2,1,0:T(1,128)S(1)}, u32[]{:S(2)}, u32[]{:S(2)}) %all-to-all-start) | async-done | bytes 262176 | tf_op jit(solution)/shard_map/all_to_all | solution.py:75
  56.3 1.3 reduce
  57.6 7.6 %reshape.36 = f32[2048,2,2,8]{3,2,1,0:T(2,128)} reshape(f32[16,4096]{1,0:T(8,128)S(1)} %reduce) | data formatting | bytes 524288
  65.2 5.1 %copy.88 = f32[16,2,2,8,128]{4,3,2,1,0:T(8,128)S(1)} copy(f32[16,2,2,8,128]{3,2,1,4,0:T(2,128)} %bitcast.43) | data formatting | bytes 524288 | tf_op jit(solution)/shard_map/all_to_all | solution.py:75
  70.4 23.6 %while.38 = (s32[]{:T(128)}, f32[8,128]{1,0:T(8,128)S(1)}, f32[8,128]{1,0:T(8,128)S(1)}, f32[8,128]{1,0:T(8,128)S(1)}, f32[2,8,128]{2,1,0:T(8,128)S(1)}, /*index...) while((s32[]{:T(128)}, f32[8,128]{1,0:T(8,128)S(1)}, ...), condition=%wide.region_1.2_spmd.clone, body=%wide.region_0.1_spmd.clone.sunk | while | flops 14339 | bytes 82048 | solution.py:55
  70.4 0.7 bitcast_dynamic-update-slice_fusion.6
  71.9 0.7 bitcast_dynamic-update-slice_fusion.6
  72.6 0.7 bitcast_dynamic-update-slice_fusion.6
  73.4 0.7 bitcast_dynamic-update-slice_fusion.6
  74.9 0.7 bitcast_dynamic-update-slice_fusion.6
  75.6 0.7 bitcast_dynamic-update-slice_fusion.6
  76.3 0.7 bitcast_dynamic-update-slice_fusion.6
  77.8 0.7 bitcast_dynamic-update-slice_fusion.6
  89.6 0.7 bitcast_dynamic-update-slice_fusion.6
  94.1 1.7 while.39
  95.8 0.7 fusion.15
  96.5 5.4 %all-to-all-start.1 = ((f32[32,2,8,128]{3,2,1,0:T(8,128)}), f32[32,2,8,128]{3,2,1,0:T(8,128)S(1)}, u32[]{:S(2)}, u32[]{:S(2)}) async-start(f32[32,2,8,128]{3,2,1,0:T(8,128)} %get-tuple-element.243), calls=%async_computation.1 | async-start | bytes 524288 | tf_op jit(solution)/shard_map/all_to_all | solution.py:77
  102.0 42.2 %all_gather.3 = f32[8,2048]{1,0:T(8,128)S(1)} all-gather(f32[8,128]{1,0:T(8,128)S(1)} %broadcast_multiply_fusion.1), channel_id=1, replica_groups=mesh['tile'=48,'layer'=16] {'layer'}, dimensions={1}, use_global_device_ids=true | all-gather | bytes 69632 | tf_op jit(solution)/shard_map/all_gather | solution.py:83
  144.2 34.3 %gather_fusion = f32[6144]{0:T(1024)S(1)} fusion(f32[16384]{0:T(1024)S(1)} %bitcast.41, s32[6144]{0:T(1024)S(1)} %broadcast_clamp_fusion), kind=kCustom, calls=%fused_computation | custom fusion | bytes 73728 | tf_op jit(solution)/shard_map/gather | solution.py:92
  179.0 8.4 %gather_fusion.1 = f32[1536]{0:T(1024)S(1)} fusion(f32[1536]{0:T(1024)S(1)} %dynamic_update_slice.20, s32[2048]{0:T(1024)S(1)} %pad_clamp_fusion), kind=kCustom, calls=%fused_computation.1 | custom fusion | bytes 18432 | tf_op jit(solution)/shard_map/gather | solution.py:101
  187.8 119.9 %all-reduce.1 = f32[768,2]{1,0:T(8,128)S(1)} all-reduce(f32[768,2]{1,0:T(8,128)S(1)} %reshape.15), channel_id=2, replica_groups=mesh['tile'=48,'layer'=16] {'tile','layer'}, use_global_device_ids=true, to_apply=%region_7.8.clone | all-reduce | flops 1536 | bytes 12288
  308.2 0.7 copy.98
  (190 shorter events, 19.6 us)
Async XLA Ops:
  1.8 14.4 %collective-permute-start = (f32[2,2,1,2048]{3,1,2,0:T(2,128)S(1)}, f32[2,2,1,2048]{3,1,2,0:T(2,128)S(1)}, u32[]{:S(2)}, u32[]{:S(2)}) collective-permute-start(f32[2,2,1,2048]{3,1,2,0:T(2,128)S(1)} %copy.94), channel_id=1, source_target_pairs={{16,0},{32,16},{48,32},{64,48},{80,64},{96,80},{112,96},{128,112},... | collective-permute-start | bytes 98312 | tf_op jit(solution)/shard_map/ppermute | solution.py:20
  14.2 3.1 %collective-permute-start.1 = (f32[2,2,1,2048]{3,1,2,0:T(2,128)S(1)}, f32[2,2,1,2048]{3,1,2,0:T(2,128)S(1)}, u32[]{:S(2)}, u32[]{:S(2)}) collective-permute-start(f32[2,2,1,2048]{3,1,2,0:T(2,128)S(1)} %copy.95), channel_id=1, source_target_pairs={{0,16},{16,32},{32,48},{48,64},{64,80},{80,96},{96,112},{112,128},... | collective-permute-start | bytes 98312 | tf_op jit(solution)/shard_map/ppermute | solution.py:17
  20.5 22.1 %copy-start.3 = (s32[8,128]{1,0:T(8,128)S(1)}, s32[8,128]{1,0:T(8,128)}, u32[]{:S(2)}) copy-start(s32[8,128]{1,0:T(8,128)} %param.17) | copy-start | bytes 12292
  20.5 22.1 %copy-start.1 = (s32[96,64]{0,1:T(8,128)S(1)}, s32[96,64]{0,1:T(8,128)}, u32[]{:S(2)}) copy-start(s32[96,64]{0,1:T(8,128)} %param.18) | copy-start | bytes 73732
  20.6 22.2 %copy-start.2 = (s32[1536]{0:T(1024)S(1)}, s32[1536]{0:T(1024)}, u32[]{:S(2)}) copy-start(s32[1536]{0:T(1024)} %param.19) | copy-start | bytes 18436
  33.8 22.0 %all-to-all-start = ((f32[16,1,4096]{2,1,0:T(1,128)}), f32[16,1,4096]{2,1,0:T(1,128)S(1)}, u32[]{:S(2)}, u32[]{:S(2)}) async-start(f32[16,1,4096]{2,1,0:T(1,128)} %reshape.35), calls=%async_computation | async-start | bytes 524288 | tf_op jit(solution)/shard_map/all_to_all | solution.py:75
  57.6 12.8 %copy-start = (f32[8,128]{1,0:T(8,128)S(1)}, f32[8,128]{1,0:T(8,128)}, u32[]{:S(2)}) copy-start(f32[8,128]{1,0:T(8,128)} %param.16) | copy-start | bytes 12292
  96.5 211.6 %all-to-all-start.1 = ((f32[32,2,8,128]{3,2,1,0:T(8,128)}), f32[32,2,8,128]{3,2,1,0:T(8,128)S(1)}, u32[]{:S(2)}, u32[]{:S(2)}) async-start(f32[32,2,8,128]{3,2,1,0:T(8,128)} %get-tuple-element.243), calls=%async_computation.1 | async-start | bytes 524288 | tf_op jit(solution)/shard_map/all_to_all | solution.py:77
where the time goes:
time: 311 us; the launch traced here: 309 us
  blocking collectives  162 us (52%)
  local copies, waits for them, and re-layouts  72.9 us (23%)
  other arithmetic  33.4 us (11%)
  starting transfers between devices  28.5 us (9%)
  waiting for transfers between devices  9.06 us (3%)
    unnamed x1, blocking collectives  120 us
    all_gather x1, blocking collectives, local(): tile_table = lax.all_gather(discharge, 'layer', axis=1, tiled=True)  42.2 us
    gather x2, local copies, waits for them, and re-layouts, local(): picked = jnp.where(inside, tile_table.reshape(-1)[local_index], 0.0)  34.4 us
    dynamic_update_slice x96, other arithmetic, column_solve(): _, (ratios, scaled) = lax.scan(forward, initial, (vertical, rhs))  23 us
    unnamed x15, local copies, waits for them, and re-layouts  17.2 us
    ppermute x1, starting transfers between devices, extended(): lax.ppermute(lax.slice_in_dim(block, 0, width, axis=dim), axis, backward)  12.4 us
    all_to_all x1, starting transfers between devices, local(): lax.all_to_all(rhs, 'layer', split_axis=3, concat_axis=0, tiled=True)  8.79 us
    gather x1, local copies, waits for them, and re-layouts, local(): owner_table = whole_list[owner_order(gate_owner)]  8.38 us
  transfers between devices with their start and end apart: 4, of which 2 were waited for; matrix products, arithmetic and copies ran while one was open for 16% of the time, Pallas kernels for 0%

commit v1 on v0

v1 whole, which is shorter than its diff:
```python
import functools

import jax
import jax.numpy as jnp
from jax import lax
from jax.experimental import pallas as pl
from jax.experimental.pallas import tpu as pltpu
from jax.sharding import PartitionSpec as P

MESH = pl.DeviceIdType.MESH
SCALE = 0.2
F32 = jnp.float32


def remote(src, dst, send_sem, recv_sem, axis, peer):
    return pltpu.make_async_remote_copy(
        src_ref=src,
        dst_ref=dst,
        send_sem=send_sem,
        recv_sem=recv_sem,
        device_id={axis: peer},
        device_id_type=MESH,
    )


def kernel(
    tiles,
    layers,
    adjoint_in,
    source_in,
    viscosity_in,
    vertical_in,
    friction_in,
    mask_in,
    cells_in,
    owner_in,
    out,
    flux,
    adjoint,
    source,
    viscosity,
    vertical,
    friction,
    mask,
    cells,
    owner,
    halo,
    rhs,
    gathered,
    solved,
    inverse,
    ratio,
    table,
    select,
    block_cells,
    cell_rows_out,
    cell_rows_in,
    gate_rows,
    picked,
    parts,
    load_sem,
    halo_send,
    halo_recv,
    rhs_send,
    rhs_recv,
    back_send,
    back_recv,
    table_send,
    table_recv,
    own_send,
    own_recv,
    rows_send,
    rows_recv,
    part_send,
    part_recv,
    self_sem,
):
    tile = lax.axis_index("tile")
    layer = lax.axis_index("layer")
    nz = vertical.shape[0]
    per_layer = nz // layers
    width = rhs.shape[3]
    rows = rhs.shape[2]

    def ring(axis, me, size, step):
        return lax.rem(me + step, size)

    barrier = pltpu.get_barrier_semaphore()

    def greet(axis, me, size):
        def one(step, carry):
            pl.semaphore_signal(
                barrier, inc=1, device_id={axis: lax.rem(me + step, size)}, device_id_type=MESH
            )
            return carry

        lax.fori_loop(1, size, one, 0)

    greet("layer", layer, layers)
    greet("tile", tile, tiles)

    loads = []
    for i, (a, b) in enumerate(
        (
            (adjoint_in, adjoint),
            (source_in, source),
            (viscosity_in, viscosity),
            (vertical_in, vertical),
            (friction_in, friction),
            (mask_in, mask),
            (cells_in, cells),
            (owner_in, owner),
        )
    ):
        copy = pltpu.make_async_copy(a, b, load_sem.at[i])
        copy.start()
        loads.append(copy)

    loads[0].wait()
    pl.semaphore_wait(barrier, layers - 1 + tiles - 1)

    up, down = lax.rem(tile + tiles - 1, tiles), lax.rem(tile + 1, tiles)
    to_down = remote(
        adjoint.at[:, :, pl.ds(rows - 1, 1)], halo.at[0], halo_send.at[0], halo_recv.at[0], "tile", down
    )
    to_up = remote(
        adjoint.at[:, :, pl.ds(0, 1)], halo.at[1], halo_send.at[1], halo_recv.at[1], "tile", up
    )
    to_down.start()
    to_up.start()

    for c in loads[1:]:
        c.wait()
    lane = lax.broadcasted_iota(jnp.int32, (1, width), 1)
    first_col, last_col = lane == 0, lane == width - 1
    sub = lax.broadcasted_iota(jnp.int32, (rows, 1), 0)

    def sideways(a):
        left = jnp.where(first_col, 0.0, pltpu.roll(a, 1, 1))
        right = jnp.where(last_col, 0.0, pltpu.roll(a, width - 1, 1))
        return left, right

    for k in range(per_layer):
        coef = SCALE * viscosity[k]
        value, diff, flat = [], [], []
        for c in range(2):
            a = adjoint[k, c]
            left, right = sideways(a)
            value.append(a)
            diff.append(0.25 * (right - left))
            flat.append(left + right - 4.0 * a)
        for c in range(2):
            above = jnp.where(sub == 0, 0.0, pltpu.roll(value[c] - diff[1 - c], 1, 0))
            below = jnp.where(sub == rows - 1, 0.0, pltpu.roll(value[c] + diff[1 - c], rows - 1, 0))
            rhs[k, c] = source[k, c] + coef * (flat[c] + (above + below))

    count = cells.shape[0]
    gates = owner.shape[0] * 128
    owner_ids = tile * layers + lax.broadcasted_iota(jnp.int32, (layers, 128), 0)
    lane128 = lax.broadcasted_iota(jnp.int32, (layers, 128), 1)
    far = jnp.full((layers, 128), gates, jnp.int32)
    for j in range(owner.shape[0]):
        mine = owner[pl.ds(j, 1), :] == owner_ids
        far = jnp.minimum(far, jnp.where(mine, lane128 + j * 128, gates))
    first = jnp.min(far, axis=1, keepdims=True)
    for j in range(owner.shape[0]):
        mine = owner[pl.ds(j, 1), :] == owner_ids
        is_first = (lane128 + j * 128) == first
        select[0:layers, j * 128 : (j + 1) * 128] = jnp.where(mine & is_first, 1.0, 0.0)
        select[layers : 2 * layers, j * 128 : (j + 1) * 128] = jnp.where(
            mine & jnp.logical_not(is_first), 1.0, 0.0
        )
    select[:, gates:] = jnp.zeros((2 * layers, select.shape[1] - gates), F32)
    base = (layer * count) // 128
    shift = layer * count - base * 128
    block_cells[...] = jnp.zeros_like(block_cells)
    block_cells[pl.ds(pl.multiple_of(shift, 32), count), :] = cells[...].astype(F32)
    chosen = jnp.dot(
        select[:, pl.ds(pl.multiple_of(base * 128, 128), 256)],
        block_cells[...],
        precision=lax.Precision.HIGHEST,
        preferred_element_type=F32,
    )
    cell_rows_out[...] = jnp.concatenate([chosen[0:layers], chosen[layers:]], axis=1)

    def own_copy(step):
        peer = lax.rem(layer + step, layers)
        return remote(
            cell_rows_out.at[pl.ds(peer, 1)],
            cell_rows_in.at[pl.ds(layer, 1)],
            own_send.at[step - 1],
            own_recv.at[step - 1],
            "layer",
            peer,
        )

    def each(size, fn):
        def one(step, carry):
            fn(step)
            return carry

        lax.fori_loop(1, size, one, 0)

    to_down.wait_recv()
    to_up.wait_recv()
    has_up, has_down = tile > 0, tile < tiles - 1
    lane_w = lax.broadcasted_iota(jnp.int32, (1, width), 1)
    for k in range(per_layer):
        top_coef = SCALE * viscosity[k, 0:1]
        low_coef = SCALE * viscosity[k, rows - 1 : rows]
        for c in range(2):
            o = 1 - c
            left, right = sideways(halo[0, k, o])
            above = halo[0, k, c] - 0.25 * (right - left)
            rhs[k, c, 0:1] += jnp.where(has_up, top_coef * above, 0.0)
            left, right = sideways(halo[1, k, o])
            below = halo[1, k, c] + 0.25 * (right - left)
            rhs[k, c, rows - 1 : rows] += jnp.where(has_down, low_coef * below, 0.0)

    def rhs_copy(step):
        peer = lax.rem(layer + step, layers)
        return remote(
            rhs.at[:, :, :, pl.ds(pl.multiple_of(peer * 128, 128), 128)],
            gathered.at[pl.ds(layer * per_layer, per_layer)],
            rhs_send.at[step - 1],
            rhs_recv.at[step - 1],
            "layer",
            peer,
        )

    each(layers, lambda s: rhs_copy(s).start())
    each(layers, lambda s: own_copy(s).start())
    for k in range(per_layer):
        for c in range(2):
            gathered[layer * per_layer + k, c] = rhs[
                k, c, :, pl.ds(pl.multiple_of(layer * 128, 128), 128)
            ]
    cell_rows_in[pl.ds(layer, 1)] = cell_rows_out[pl.ds(layer, 1)]

    active = mask[...].astype(F32)
    beneath = friction[...]
    link = jnp.zeros_like(beneath)
    ratio_prev = jnp.zeros_like(beneath)
    for k in range(nz):
        v = vertical[k]
        inv = 1.0 / (1.0 + beneath + v - link * ratio_prev)
        ratio_prev = v * inv
        inverse[k] = inv
        ratio[k] = ratio_prev
        beneath = v
        link = v

    each(layers, lambda s: own_copy(s).wait_recv())
    gate_rows[pl.ds(tile, 1)] = jnp.sum(cell_rows_in[...], axis=0, keepdims=True)

    def rows_copy(step):
        return remote(
            gate_rows.at[pl.ds(tile, 1)],
            gate_rows.at[pl.ds(tile, 1)],
            rows_send.at[step - 1],
            rows_recv.at[step - 1],
            "tile",
            lax.rem(tile + step, tiles),
        )

    each(tiles, lambda s: rows_copy(s).start())

    each(layers, lambda s: rhs_copy(s).wait_recv())
    scaled = [jnp.zeros((rows, 128), F32)] * 2
    for k in range(nz):
        inv = inverse[k]
        for c in range(2):
            if k:
                scaled[c] = (gathered[k, c] + vertical[k - 1] * scaled[c]) * inv
            else:
                scaled[c] = gathered[k, c] * inv
            solved[k, c] = scaled[c]
    upper = [jnp.zeros((rows, 128), F32)] * 2
    total = jnp.zeros((rows, 128), F32)
    for k in reversed(range(nz)):
        for c in range(2):
            upper[c] = solved[k, c] + ratio[k] * upper[c] if k < nz - 1 else solved[k, c]
            x = upper[c] * active
            solved[k, c] = x
            total = total + x
    table[layer] = total * (1.0 / nz)

    def table_copy(step):
        return remote(
            table.at[layer],
            table.at[layer],
            table_send.at[step - 1],
            table_recv.at[step - 1],
            "layer",
            lax.rem(layer + step, layers),
        )

    each(layers, lambda s: table_copy(s).start())

    def back_copy(step):
        peer = lax.rem(layer + step, layers)
        return remote(
            solved.at[pl.ds(peer * per_layer, per_layer)],
            out.at[:, :, :, pl.ds(pl.multiple_of(layer * 128, 128), 128)],
            back_send.at[step - 1],
            back_recv.at[step - 1],
            "layer",
            peer,
        )

    each(layers, lambda s: back_copy(s).start())
    keep = pltpu.make_async_copy(
        solved.at[pl.ds(layer * per_layer, per_layer)],
        out.at[:, :, :, pl.ds(pl.multiple_of(layer * 128, 128), 128)],
        self_sem,
    )
    keep.start()

    each(tiles, lambda s: rows_copy(s).wait_recv())
    where, lanes = [], []
    groups = tiles // 8
    for v in range(groups):
        cell = gate_rows[v * 8 : (v + 1) * 8].astype(jnp.int32)
        row, col = cell // width, cell % width
        here = (row // rows) == tile
        where.append(jnp.where(here, (col // 128) * rows + row % rows, -1))
        lanes.append(col % 128)

    each(layers, lambda s: table_copy(s).wait_recv())
    found = [jnp.zeros((8, 128), F32)] * groups
    for l in range(layers):
        for r in range(rows):
            line = jnp.broadcast_to(table[l, r : r + 1], (8, 128))
            for v in range(groups):
                got = jnp.take_along_axis(line, lanes[v], axis=1, mode="promise_in_bounds")
                found[v] = jnp.where(where[v] == l * rows + r, got, found[v])
    for v in range(groups):
        picked[v * 8 : (v + 1) * 8] = found[v]

    def part_copy(step):
        peer = lax.rem(tile + step, tiles)
        return remote(
            picked.at[pl.ds(peer, 1)],
            parts.at[pl.ds(tile, 1)],
            part_send.at[step - 1],
            part_recv.at[step - 1],
            "tile",
            peer,
        )

    each(tiles, lambda s: part_copy(s).start())
    parts[pl.ds(tile, 1)] = picked[pl.ds(tile, 1)]
    each(tiles, lambda s: part_copy(s).wait_recv())
    line = jnp.sum(parts[...], axis=0, keepdims=True)
    half = lax.broadcasted_iota(jnp.int32, (1, 128), 1) < 64
    low = jnp.sum(jnp.where(half, line, 0.0), axis=1, keepdims=True)
    high = jnp.sum(jnp.where(half, 0.0, line), axis=1, keepdims=True)
    flux[...] = jnp.where(lax.broadcasted_iota(jnp.int32, (1, 2), 1) == 0, low, high)

    each(layers, lambda s: back_copy(s).wait_recv())
    keep.wait()
    to_down.wait_send()
    to_up.wait_send()

    def sent(step):
        own_copy(step).wait_send()
        rhs_copy(step).wait_send()
        table_copy(step).wait_send()
        back_copy(step).wait_send()

    each(layers, sent)

    def sent_tile(step):
        rows_copy(step).wait_send()
        part_copy(step).wait_send()

    each(tiles, sent_tile)


def solution(mesh):
    tiles, layers = mesh.shape["tile"], mesh.shape["layer"]

    def local(adjoint, source, viscosity, vertical, friction, ice_mask, gate_cells, gate_owner):
        owner = gate_owner.reshape(-1, 128)
        per_layer, _, rows, width = adjoint.shape
        nz = vertical.shape[0]
        vmem, dma = pltpu.VMEM, pltpu.SemaphoreType.DMA
        scratch = [
            vmem(a.shape, a.dtype)
            for a in (adjoint, source, viscosity, vertical, friction, ice_mask, gate_cells, owner)
        ]
        scratch += [
            vmem((2, per_layer, 2, 1, width), F32),
            vmem(adjoint.shape, F32),
            vmem((nz, 2, rows, 128), F32),
            vmem((nz, 2, rows, 128), F32),
            vmem((nz, rows, 128), F32),
            vmem((nz, rows, 128), F32),
            vmem((layers, rows, 128), F32),
            vmem((2 * layers, owner.size + 128), F32),
            vmem((256, gate_cells.shape[1]), F32),
            vmem((layers, 128), F32),
            vmem((layers, 128), F32),
            vmem((tiles, 128), F32),
            vmem((tiles, 128), F32),
            vmem((tiles, 128), F32),
            dma((8,)),
        ]
        for n in (2, layers - 1, layers - 1, layers - 1, layers - 1, tiles - 1, tiles - 1):
            scratch += [dma((n,)), dma((n,))]
        scratch += [dma]
        return pl.pallas_call(
            functools.partial(kernel, tiles, layers),
            out_shape=(
                jax.ShapeDtypeStruct(adjoint.shape, F32),
                jax.ShapeDtypeStruct((1, 2), F32),
            ),
            in_specs=[pl.BlockSpec(memory_space=pl.ANY)] * 8,
            out_specs=(
                pl.BlockSpec(memory_space=pl.ANY),
                pl.BlockSpec(memory_space=pltpu.VMEM),
            ),
            scratch_shapes=scratch,
            compiler_params=pltpu.CompilerParams(
                collective_id=0, has_side_effects=True, vmem_limit_bytes=32 * 1024 * 1024
            ),
            name="update",
        )(adjoint, source, viscosity, vertical, friction, ice_mask, gate_cells, owner)

    return jax.shard_map(
        local,
        mesh=mesh,
        in_specs=(
            P("layer", None, "tile", None),
            P("layer", None, "tile", None),
            P("layer", "tile", None),
            P(None, "tile", "layer"),
            P("tile", "layer"),
            P("tile", "layer"),
            P("layer", None),
            P(),
        ),
        out_specs=(P("layer", None, "tile", None), P(("tile", "layer"), None)),
        check_vma=False,
    )
```

time: 311 us -> 70.1 us (0.23)
  blocking collectives: 162 us -> 0 us
  local copies, waits for them, and re-layouts: 72.9 us -> 5.79 us
  Pallas kernels: 0 us -> 63.3 us
  other arithmetic: 33.4 us -> 0 us
  starting transfers between devices: 28.5 us -> 0 us
  waiting for transfers between devices: 9.06 us -> 0 us
    unnamed x1 -> x0, blocking collectives: 120 us -> none
    pallas_call x0 -> x1, Pallas kernels: none -> 63.3 us  [local(): pl.pallas_call(functools.partial(kernel, tiles, layers), out_shape=(jax.S...]
    gather x3 -> x0, local copies, waits for them, and re-layouts: 42.7 us -> none  [the longest x2 34.4 us: local(): picked = jnp.where(inside, tile_table.reshape(-1)[local_index], 0.0)]
    all_gather x1 -> x0, blocking collectives: 42.2 us -> none  [local(): tile_table = lax.all_gather(discharge, 'layer', axis=1, tiled=True)]
    dynamic_update_slice x96 -> x0, other arithmetic: 23 us -> none  [column_solve(): _, (ratios, scaled) = lax.scan(forward, initial, (vertical, rhs))]
    ppermute x2 -> x0, starting transfers between devices: 14.3 us -> none  [the longest x1 12.4 us: extended(): lax.ppermute(lax.slice_in_dim(block, 0, width, axis=dim), axis, backward)]
    all_to_all x2 -> x0, starting transfers between devices: 14.2 us -> none  [the longest x1 8.79 us: local(): lax.all_to_all(rhs, 'layer', split_axis=3, concat_axis=0, tiled=True)]
    unnamed x15 -> x17, local copies, waits for them, and re-layouts: 17.2 us -> 5.79 us
  transfers between devices with their start and end apart: 4 -> 0, of which waited for: 2 -> 0; matrix products, arithmetic and copies ran while one was open for 16% -> 0% of each run, Pallas kernels for 0% -> 0%
where the time goes in v1:
time: 70.1 us; the launch traced here: 69.8 us
  Pallas kernels  63.3 us (90%)
  local copies, waits for them, and re-layouts  5.79 us (8%)
    pallas_call x1, Pallas kernels, local(): pl.pallas_call(functools.partial(kernel, tiles, layers), out_shape=(jax.S...  63.3 us
    unnamed x17, local copies, waits for them, and re-layouts  5.79 us

profile of v1, /device:TPU:1, one launch (start us, length us, event | category | flops | bytes accessed | tf_op | source)
XLA Modules:
  0.0 69.8 jit_solution(5850527582695883266)
XLA Ops:
  0.6 0.0 copy-start.4
  0.6 0.0 copy-start.5
  0.7 0.0 copy-start.6
  0.7 0.9 %copy.10.cells_in = s32[96,64]{1,0:T(8,128)S(1)} copy(s32[96,64]{0,1:T(8,128)} %param.14) | data formatting | bytes 49152 | tf_op args[6]
  1.5 0.0 copy-done.4
  1.5 0.0 copy-done.5
  1.5 0.0 copy-done.6
  1.6 0.0 copy-start
  1.6 0.9 %copy-done = f32[2,2,8,2048]{3,2,1,0:T(8,128)S(1)} copy-done((f32[2,2,8,2048]{3,2,1,0:T(8,128)S(1)}, f32[2,2,8,2048]{3,2,1,0:T(8,128)}, u32[]{:S(2)}) %copy-start) | copy-done | bytes 262168
  2.5 0.0 copy-start.1
  2.5 0.9 %copy-done.1 = f32[2,2,8,2048]{3,2,1,0:T(8,128)S(1)} copy-done((f32[2,2,8,2048]{3,2,1,0:T(8,128)S(1)}, f32[2,2,8,2048]{3,2,1,0:T(8,128)}, u32[]{:S(2)}) %copy-start.1) | copy-done | bytes 262168
  3.5 0.0 copy-start.2
  3.5 0.9 %copy-done.2 = f32[2,8,2048]{2,1,0:T(8,128)S(1)} copy-done((f32[2,8,2048]{2,1,0:T(8,128)S(1)}, f32[2,8,2048]{2,1,0:T(8,128)}, u32[]{:S(2)}) %copy-start.2) | copy-done | bytes 131096
  4.4 0.0 copy-start.3
  4.4 0.9 %copy-done.3 = f32[32,8,128]{2,1,0:T(8,128)S(1)} copy-done((f32[32,8,128]{2,1,0:T(8,128)S(1)}, f32[32,8,128]{2,1,0:T(8,128)}, u32[]{:S(2)}) %copy-start.3) | copy-done | bytes 131096
  5.3 63.3 %update.1 = (f32[2,2,8,2048]{3,2,1,0:T(8,128)S(1)}, f32[1,2]{1,0:T(1,128)S(1)}) custom-call(f32[2,2,8,2048]{3,2,1,0:T(8,128)S(1)} %copy-done, f32[2,2,8,2048]{3,2,1,0:T(8,128)S(1)} %copy-done.1, f32[2,8,2048]{2,1,0:T(8,128)S(1)} %copy-done.2, f32[32,8,128]{2,1,0:T(8,128)S(1)} %copy-done.3, f32[8,128]{1,0:T(8,128)S(1)} %copy-done.5, s32[8,128]{1,0:T(8,128)S(1)} %copy-done.6, ...), custom_call_target="tpu_custom_call" | custom-call | tf_op jit(solution)/shard_map/update/pallas_call | solution.py:412
  68.6 0.7 %copy.13 = f32[2,2,8,2048]{3,2,1,0:T(8,128)} copy(f32[2,2,8,2048]{3,2,1,0:T(8,128)S(1)} %get-tuple-element.4) | data formatting | bytes 524288
  69.3 0.5 copy.14
Async XLA Ops:
  0.6 0.9 %copy-start.4 = (s32[1536]{0:T(1024)S(1)}, s32[1536]{0:T(1024)}, u32[]{:S(2)}) copy-start(s32[1536]{0:T(1024)} %param.15) | copy-start | bytes 18436
  0.6 0.9 %copy-start.5 = (f32[8,128]{1,0:T(8,128)S(1)}, f32[8,128]{1,0:T(8,128)}, u32[]{:S(2)}) copy-start(f32[8,128]{1,0:T(8,128)} %friction_in.1) | copy-start | bytes 12292
  0.7 0.9 %copy-start.6 = (s32[8,128]{1,0:T(8,128)S(1)}, s32[8,128]{1,0:T(8,128)}, u32[]{:S(2)}) copy-start(s32[8,128]{1,0:T(8,128)} %mask_in.1) | copy-start | bytes 12292
  1.6 1.0 %copy-start = (f32[2,2,8,2048]{3,2,1,0:T(8,128)S(1)}, f32[2,2,8,2048]{3,2,1,0:T(8,128)}, u32[]{:S(2)}) copy-start(f32[2,2,8,2048]{3,2,1,0:T(8,128)} %adjoint_in.1) | copy-start | bytes 786436
  2.5 0.9 %copy-start.1 = (f32[2,2,8,2048]{3,2,1,0:T(8,128)S(1)}, f32[2,2,8,2048]{3,2,1,0:T(8,128)}, u32[]{:S(2)}) copy-start(f32[2,2,8,2048]{3,2,1,0:T(8,128)} %source_in.1) | copy-start | bytes 786436
  3.5 0.9 %copy-start.2 = (f32[2,8,2048]{2,1,0:T(8,128)S(1)}, f32[2,8,2048]{2,1,0:T(8,128)}, u32[]{:S(2)}) copy-start(f32[2,8,2048]{2,1,0:T(8,128)} %viscosity_in.1) | copy-start | bytes 393220
  4.4 0.9 %copy-start.3 = (f32[32,8,128]{2,1,0:T(8,128)S(1)}, f32[32,8,128]{2,1,0:T(8,128)}, u32[]{:S(2)}) copy-start(f32[32,8,128]{2,1,0:T(8,128)} %vertical_in.1) | copy-start | bytes 393220

commit v2 on v1

v2 whole, which is shorter than its diff:
```python
import functools

import jax
import jax.numpy as jnp
from jax import lax
from jax.experimental import pallas as pl
from jax.experimental.pallas import tpu as pltpu
from jax.sharding import PartitionSpec as P

MESH = pl.DeviceIdType.MESH
SCALE = 0.2
F32 = jnp.float32


NX, NY, ZLO, ZHI, NC = 4, 8, 3, 4, 2


def remote(src, dst, send_sem, recv_sem, device):
    return pltpu.make_async_remote_copy(
        src_ref=src,
        dst_ref=dst,
        send_sem=send_sem,
        recv_sem=recv_sem,
        device_id=device,
        device_id_type=MESH,
    )


def kernel(
    tiles,
    layers,
    adjoint_in,
    source_in,
    viscosity_in,
    vertical_in,
    friction_in,
    mask_in,
    cells_in,
    owner_in,
    out,
    flux,
    adjoint,
    source,
    viscosity,
    vertical,
    friction,
    mask,
    cells,
    owner,
    halo,
    rhs,
    edge,
    gathered,
    edges_in,
    solved,
    inverse,
    ratio,
    table,
    select,
    block_cells,
    cell_rows_out,
    cell_rows_in,
    gate_rows,
    picked,
    parts,
    load_sem,
    halo_send,
    halo_recv,
    rhs_send,
    rhs_recv,
    edge_send,
    edge_recv,
    back_send,
    back_recv,
    own_send,
    own_recv,
    table_send,
    table_recv,
    rows_send,
    rows_recv,
    part_send,
    part_recv,
    self_sem,
    halo_ready,
    layer_ready,
    late_ready,
):
    tile = lax.axis_index("tile")
    layer = lax.axis_index("layer")
    nz = vertical.shape[0]
    per_layer = nz // layers
    width = rhs.shape[3]
    rows = rhs.shape[2]
    core, y, z_lo = tile % NC, (tile // NC) % NY, tile // (NC * NY)
    x, z_hi = layer % NX, layer // NX
    xy = y * NX + x
    zc = (z_hi * ZLO + z_lo) * NC + core
    n_xy, n_zc = NX * NY, ZHI * ZLO * NC
    y_rank = jnp.where(y < NY // 2, y, NY + NY // 2 - 1 - y)

    def loop(low, high, fn):
        def one(i, carry):
            fn(i)
            return carry

        lax.fori_loop(low, high, one, 0)

    def at_xy(q):
        qy, qx = q // NX, q % NX
        return {"tile": (z_lo * NY + qy) * NC + core, "layer": z_hi * NX + qx}

    def at_zc(q):
        qc, qz = q % NC, q // NC
        return {"tile": ((qz % ZLO) * NY + y) * NC + qc, "layer": (qz // ZLO) * NX + x}

    def at_layer(p):
        return {"tile": tile, "layer": p}

    def other_y(q):
        return q // NX != y

    def other_zc(q):
        return jnp.logical_or(q % NC != core, (q // NC) % ZLO != z_lo)

    def signal(sem, device):
        pl.semaphore_signal(sem, inc=1, device_id=device, device_id_type=MESH)

    loads = []
    for i, (a, b) in enumerate(
        (
            (adjoint_in, adjoint),
            (source_in, source),
            (viscosity_in, viscosity),
            (vertical_in, vertical),
            (friction_in, friction),
            (mask_in, mask),
            (cells_in, cells),
            (owner_in, owner),
        )
    ):
        copy = pltpu.make_async_copy(a, b, load_sem.at[i])
        copy.start()
        loads.append(copy)

    barrier = pltpu.get_barrier_semaphore()
    has_up, has_down = tile > 0, tile < tiles - 1

    @pl.when(has_down)
    def _():
        signal(barrier, {"tile": tile + 1, "layer": layer})

    loop(layer + 1, layers, lambda p: signal(barrier, at_layer(p)))

    def greet_xy(q):
        qy = q // NX
        rank = jnp.where(qy < NY // 2, qy, NY + NY // 2 - 1 - qy)

        @pl.when(rank > y_rank)
        def _():
            signal(barrier, at_xy(q))

    loop(0, n_xy, greet_xy)

    def greet_zc(q):
        @pl.when(other_zc(q))
        def _():
            signal(barrier, at_zc(q))

    loop(zc + 1, n_zc, greet_zc)

    for c in loads:
        c.wait()
    lane = lax.broadcasted_iota(jnp.int32, (1, width), 1)
    first_col, last_col = lane == 0, lane == width - 1
    sub = lax.broadcasted_iota(jnp.int32, (rows, 1), 0)

    def sideways(a):
        left = jnp.where(first_col, 0.0, pltpu.roll(a, 1, 1))
        right = jnp.where(last_col, 0.0, pltpu.roll(a, width - 1, 1))
        return left, right

    for k in range(per_layer):
        coef = SCALE * viscosity[k]
        value, diff, flat = [], [], []
        for c in range(2):
            a = adjoint[k, c]
            left, right = sideways(a)
            value.append(a)
            diff.append(0.25 * (right - left))
            flat.append(left + right - 4.0 * a)
        for c in range(2):
            above = jnp.where(sub == 0, 0.0, pltpu.roll(value[c] - diff[1 - c], 1, 0))
            below = jnp.where(sub == rows - 1, 0.0, pltpu.roll(value[c] + diff[1 - c], rows - 1, 0))
            r = source[k, c] + coef * (flat[c] + (above + below))
            rhs[k, c] = r
            edge[k, c, 0:1] = r[0:1]
            edge[k, c, 1:2] = r[rows - 1 : rows]

    count = cells.shape[1]
    gates = owner.shape[0] * 128
    owner_ids = tile * layers + lax.broadcasted_iota(jnp.int32, (layers, 128), 0)
    lane128 = lax.broadcasted_iota(jnp.int32, (layers, 128), 1)
    far = jnp.full((layers, 128), gates, jnp.int32)
    for j in range(owner.shape[0]):
        mine = owner[pl.ds(j, 1), :] == owner_ids
        far = jnp.minimum(far, jnp.where(mine, lane128 + j * 128, gates))
    first = jnp.min(far, axis=1, keepdims=True)
    for j in range(owner.shape[0]):
        mine = owner[pl.ds(j, 1), :] == owner_ids
        is_first = (lane128 + j * 128) == first
        select[0:layers, j * 128 : (j + 1) * 128] = jnp.where(mine & is_first, 1.0, 0.0)
        select[layers : 2 * layers, j * 128 : (j + 1) * 128] = jnp.where(
            mine & jnp.logical_not(is_first), 1.0, 0.0
        )
    select[:, gates:] = jnp.zeros((2 * layers, select.shape[1] - gates), F32)
    base = (layer * count) // 128
    shift = layer * count - base * 128
    block_cells[...] = jnp.zeros_like(block_cells)
    block_cells[:, 0:count] = cells[...].astype(F32)
    window = select[:, pl.ds(pl.multiple_of(base * 128, 128), 256)]
    window = pltpu.roll(window, lax.rem(256 - shift, 256), 1)[:, 0:128]
    chosen = lax.dot_general(
        window,
        block_cells[...],
        (((1,), (1,)), ((), ())),
        precision=lax.Precision.HIGHEST,
        preferred_element_type=F32,
    )
    cell_rows_out[...] = jnp.concatenate([chosen[0:layers], chosen[layers:]], axis=1)
    cell_rows_in[pl.ds(layer, 1)] = cell_rows_out[pl.ds(layer, 1)]

    active = mask[...].astype(F32)
    beneath = friction[...]
    link = jnp.zeros_like(beneath)
    ratio_prev = jnp.zeros_like(beneath)
    for k in range(nz):
        v = vertical[k]
        inv = 1.0 / (1.0 + beneath + v - link * ratio_prev)
        ratio_prev = v * inv
        inverse[k] = inv
        ratio[k] = ratio_prev
        beneath = v
        link = v

    lower = layer + y_rank * NX + zc - z_hi + has_up.astype(jnp.int32)

    @pl.when(lower > 0)
    def _():
        pl.semaphore_wait(barrier, lower)

    @pl.when(has_up)
    def _():
        signal(halo_ready, {"tile": tile - 1, "layer": layer})

    loop(0, layer, lambda p: signal(layer_ready.at[layer], at_layer(p)))

    to_down = remote(
        adjoint.at[:, :, pl.ds(rows - 1, 1)],
        halo.at[0],
        halo_send.at[0],
        halo_recv.at[0],
        {"tile": tile + 1, "layer": layer},
    )
    to_up = remote(
        adjoint.at[:, :, pl.ds(0, 1)],
        halo.at[1],
        halo_send.at[1],
        halo_recv.at[1],
        {"tile": tile - 1, "layer": layer},
    )

    @pl.when(has_up)
    def _():
        to_up.start()

    def answer_xy(q):
        qy = q // NX
        rank = jnp.where(qy < NY // 2, qy, NY + NY // 2 - 1 - qy)

        @pl.when(rank < y_rank)
        def _():
            signal(late_ready, at_xy(q))

    def answer_zc(q):
        @pl.when(other_zc(q))
        def _():
            signal(late_ready, at_zc(q))

    def rhs_copy(peer, slot):
        return remote(
            rhs.at[:, :, pl.ds(1, rows - 2), pl.ds(pl.multiple_of(peer * 128, 128), 128)],
            gathered.at[pl.ds(layer * per_layer, per_layer), :, pl.ds(1, rows - 2)],
            rhs_send.at[peer],
            rhs_recv.at[slot],
            at_layer(peer),
        )

    def own_copy(peer, slot):
        return remote(
            cell_rows_out.at[pl.ds(peer, 1)],
            cell_rows_in.at[pl.ds(layer, 1)],
            own_send.at[peer],
            own_recv.at[slot],
            at_layer(peer),
        )

    def edge_copy(peer, slot):
        return remote(
            edge.at[:, :, :, pl.ds(pl.multiple_of(peer * 128, 128), 128)],
            edges_in.at[pl.ds(layer * per_layer, per_layer)],
            edge_send.at[peer],
            edge_recv.at[slot],
            at_layer(peer),
        )

    def send_rhs(s):
        peer = jnp.where(s <= layer, layer - s, s)

        @pl.when(s > layer)
        def _():
            pl.semaphore_wait(layer_ready.at[peer], 1)

        rhs_copy(peer, layer).start()
        own_copy(peer, layer).start()

    loop(1, layer + 1, send_rhs)
    loop(0, n_xy, answer_xy)
    loop(0, zc, answer_zc)

    @pl.when(has_down)
    def _():
        pl.semaphore_wait(halo_ready, 1)
        to_down.start()

    loop(layer + 1, layers, send_rhs)

    def beside(side, row, sign):
        for k in range(per_layer):
            factor = SCALE * viscosity[k, row : row + 1]
            for c in range(2):
                left, right = sideways(halo[side, k, 1 - c])
                term = halo[side, k, c] + (sign * 0.25) * (right - left)
                edge[k, c, side : side + 1] += factor * term

    @pl.when(has_up)
    def _():
        to_down.wait_recv()
        beside(0, 0, -1.0)

    @pl.when(has_down)
    def _():
        to_up.wait_recv()
        beside(1, rows - 1, 1.0)

    def other_layers(fn):
        def one(s):
            fn(lax.rem(layer + s, layers))

        loop(1, layers, one)

    other_layers(lambda p: edge_copy(p, layer).start())
    here = pl.ds(pl.multiple_of(layer * 128, 128), 128)
    for k in range(per_layer):
        for c in range(2):
            gathered[layer * per_layer + k, c] = rhs[k, c, :, here]
            edges_in[layer * per_layer + k, c] = edge[k, c, :, here]

    other_layers(lambda p: own_copy(p, p).wait_recv())
    gate_rows[pl.ds(zc, 1)] = jnp.sum(cell_rows_in[...], axis=0, keepdims=True)
    answers = (NY - 1 - y_rank) * NX + (n_zc - 1 - zc) - (ZHI - 1 - z_hi)

    @pl.when(answers > 0)
    def _():
        pl.semaphore_wait(late_ready, answers)

    def others(size, me, fn):
        def one(s):
            fn(lax.rem(me + s, size))

        loop(1, size, one)

    def rows_copy(q, slot):
        return remote(
            gate_rows.at[pl.ds(zc, 1)], gate_rows.at[pl.ds(zc, 1)], rows_send.at[q], rows_recv.at[slot], at_zc(q)
        )

    others(n_zc, zc, lambda q: rows_copy(q, zc).start())

    other_layers(lambda p: rhs_copy(p, p).wait_recv())
    other_layers(lambda p: edge_copy(p, p).wait_recv())
    row_of = lax.broadcasted_iota(jnp.int32, (rows, 128), 0)
    top, low = row_of == 0, row_of == rows - 1
    scaled = [jnp.zeros((rows, 128), F32)] * 2
    for k in range(nz):
        inv = inverse[k]
        for c in range(2):
            r = jnp.where(low, edges_in[k, c, 1:2], gathered[k, c])
            r = jnp.where(top, edges_in[k, c, 0:1], r)
            scaled[c] = (r + vertical[k - 1] * scaled[c]) * inv if k else r * inv
            solved[k, c] = scaled[c]
    upper = [jnp.zeros((rows, 128), F32)] * 2
    total = jnp.zeros((rows, 128), F32)
    for k in reversed(range(nz)):
        for c in range(2):
            upper[c] = solved[k, c] + ratio[k] * upper[c] if k < nz - 1 else solved[k, c]
            x_new = upper[c] * active
            solved[k, c] = x_new
            total = total + x_new
    table[xy] = total * (1.0 / nz)

    def table_copy(q, slot):
        return remote(table.at[xy], table.at[xy], table_send.at[q], table_recv.at[slot], at_xy(q))

    others(n_xy, xy, lambda q: table_copy(q, xy).start())

    def back_copy(peer, slot):
        return remote(
            solved.at[pl.ds(peer * per_layer, per_layer)],
            out.at[:, :, :, here],
            back_send.at[peer],
            back_recv.at[slot],
            at_layer(peer),
        )

    other_layers(lambda p: back_copy(p, layer).start())
    keep = pltpu.make_async_copy(solved.at[pl.ds(layer * per_layer, per_layer)], out.at[:, :, :, here], self_sem)
    keep.start()

    others(n_zc, zc, lambda q: rows_copy(q, q).wait_recv())
    groups = n_zc // 8
    where, lanes = [], []
    for v in range(groups):
        cell = gate_rows[v * 8 : (v + 1) * 8].astype(jnp.int32)
        row, col = cell // width, cell % width
        t, piece = row // rows, col // 128
        inside = (t % NC == core) & (t // (NC * NY) == z_lo) & (piece // NX == z_hi)
        spot = (((t // NC) % NY) * NX + piece % NX) * rows + row % rows
        where.append(jnp.where(inside, spot, -1))
        lanes.append(col % 128)

    def look(s, found):
        q = lax.rem(xy + s, n_xy)

        @pl.when(s > 0)
        def _():
            table_copy(q, q).wait_recv()

        found = list(found)
        for r in range(rows):
            line = jnp.broadcast_to(table[q, r : r + 1], (8, 128))
            for v in range(groups):
                got = jnp.take_along_axis(line, lanes[v], axis=1, mode="promise_in_bounds")
                found[v] = jnp.where(where[v] == q * rows + r, got, found[v])
        return tuple(found)

    found = lax.fori_loop(0, n_xy, look, tuple(jnp.zeros((8, 128), F32) for _ in range(groups)))
    for v in range(groups):
        picked[v * 8 : (v + 1) * 8] = found[v]

    def part_copy(q, slot):
        return remote(
            picked.at[pl.ds(q, 1)], parts.at[pl.ds(zc, 1)], part_send.at[q], part_recv.at[slot], at_zc(q)
        )

    others(n_zc, zc, lambda q: part_copy(q, zc).start())
    parts[pl.ds(zc, 1)] = picked[pl.ds(zc, 1)]
    others(n_zc, zc, lambda q: part_copy(q, q).wait_recv())
    line = jnp.sum(parts[...], axis=0, keepdims=True)
    half = lax.broadcasted_iota(jnp.int32, (1, 128), 1) < 64
    slot0 = jnp.sum(jnp.where(half, line, 0.0), axis=1, keepdims=True)
    slot1 = jnp.sum(jnp.where(half, 0.0, line), axis=1, keepdims=True)
    flux[...] = jnp.where(lax.broadcasted_iota(jnp.int32, (1, 2), 1) == 0, slot0, slot1)

    other_layers(lambda p: back_copy(p, p).wait_recv())
    keep.wait()

    @pl.when(has_up)
    def _():
        to_up.wait_send()

    @pl.when(has_down)
    def _():
        to_down.wait_send()

    def sent(p):
        rhs_copy(p, p).wait_send()
        edge_copy(p, p).wait_send()
        own_copy(p, p).wait_send()
        back_copy(p, p).wait_send()

    other_layers(sent)
    others(n_xy, xy, lambda q: table_copy(q, q).wait_send())

    def sent_zc(q):
        rows_copy(q, q).wait_send()
        part_copy(q, q).wait_send()

    others(n_zc, zc, sent_zc)


def solution(mesh):
    tiles, layers = mesh.shape["tile"], mesh.shape["layer"]
    n_xy, n_zc = NX * NY, ZHI * ZLO * NC
    assert tiles == ZLO * NY * NC and layers == ZHI * NX

    def local(adjoint, source, viscosity, vertical, friction, ice_mask, gate_cells, gate_owner):
        owner = gate_owner.reshape(-1, 128)
        gate_cells = gate_cells.T
        per_layer, _, rows, width = adjoint.shape
        nz = vertical.shape[0]
        vmem, dma = pltpu.VMEM, pltpu.SemaphoreType.DMA
        scratch = [
            vmem(a.shape, a.dtype)
            for a in (adjoint, source, viscosity, vertical, friction, ice_mask, gate_cells, owner)
        ]
        scratch += [
            vmem((2, per_layer, 2, 1, width), F32),
            vmem(adjoint.shape, F32),
            vmem((per_layer, 2, 2, width), F32),
            vmem((nz, 2, rows, 128), F32),
            vmem((nz, 2, 2, 128), F32),
            vmem((nz, 2, rows, 128), F32),
            vmem((nz, rows, 128), F32),
            vmem((nz, rows, 128), F32),
            vmem((n_xy, rows, 128), F32),
            vmem((2 * layers, owner.size + 128), F32),
            vmem((gate_cells.shape[0], 128), F32),
            vmem((layers, 128), F32),
            vmem((layers, 128), F32),
            vmem((n_zc, 128), F32),
            vmem((n_zc, 128), F32),
            vmem((n_zc, 128), F32),
            dma((8,)),
        ]
        for n in (2, layers, layers, layers, layers, n_xy, n_zc, n_zc):
            scratch += [dma((n,)), dma((n,))]
        plain = pltpu.SemaphoreType.REGULAR
        scratch += [dma, plain, plain((layers,)), plain]
        return pl.pallas_call(
            functools.partial(kernel, tiles, layers),
            out_shape=(
                jax.ShapeDtypeStruct(adjoint.shape, F32),
                jax.ShapeDtypeStruct((1, 2), F32),
            ),
            in_specs=[pl.BlockSpec(memory_space=pltpu.HBM)] * 8,
            out_specs=(
                pl.BlockSpec(memory_space=pl.ANY),
                pl.BlockSpec(memory_space=pltpu.VMEM),
            ),
            scratch_shapes=scratch,
            compiler_params=pltpu.CompilerParams(
                collective_id=0, has_side_effects=True, vmem_limit_bytes=60 * 1024 * 1024
            ),
            name="update",
        )(adjoint, source, viscosity, vertical, friction, ice_mask, gate_cells, owner)

    return jax.shard_map(
        local,
        mesh=mesh,
        in_specs=(
            P("layer", None, "tile", None),
            P("layer", None, "tile", None),
            P("layer", "tile", None),
            P(None, "tile", "layer"),
            P("tile", "layer"),
            P("tile", "layer"),
            P("layer", None),
            P(),
        ),
        out_specs=(P("layer", None, "tile", None), P(("tile", "layer"), None)),
        check_vma=False,
    )
```

time: 70.1 us -> 59.7 us (0.85)
  Pallas kernels: 63.3 us -> 56.8 us
  local copies, waits for them, and re-layouts: 5.79 us -> 2.19 us
    pallas_call x1, Pallas kernels: 63.3 us -> 56.8 us  [local(): pl.pallas_call(functools.partial(kernel, tiles, layers), out_shape=(jax.S...]
    unnamed x17 -> x4, local copies, waits for them, and re-layouts: 5.79 us -> 2.19 us
where the time goes in v2:
time: 59.7 us; the launch traced here: 59.6 us
  Pallas kernels  56.8 us (95%)
  local copies, waits for them, and re-layouts  2.19 us (4%)
  between operations  0.65 us (1%)
    pallas_call x1, Pallas kernels, local(): pl.pallas_call(functools.partial(kernel, tiles, layers), out_shape=(jax.S...  56.8 us
    unnamed x4, local copies, waits for them, and re-layouts  2.19 us

profile of v2, /device:TPU:1, one launch (start us, length us, event | category | flops | bytes accessed | tf_op | source)
XLA Modules:
  0.0 59.6 jit_solution(13929148190942796843)
XLA Ops:
  0.6 56.8 %update.1 = (f32[2,2,8,2048]{3,2,1,0:T(8,128)}, f32[1,2]{1,0:T(1,128)}) custom-call(f32[2,2,8,2048]{3,2,1,0:T(8,128)} %adjoint_in.1, f32[2,2,8,2048]{3,2,1,0:T(8,128)} %source_in.1, f32[2,8,2048]{2,1,0:T(8,128)} %viscosity_in.1, f32[32,8,128]{2,1,0:T(8,128)} %vertical_in.1, f32[8,128]{1,0:T(8,128)} %friction_in.1, s32[8,128]{1,0:T(8,128)} %mask_in.1, ...), custom_call_target="tpu_custom_call" | custom-call | tf_op jit(solution)/shard_map/update/pallas_call | solution.py:539
  57.4 0.0 copy-start
  57.4 1.7 %copy.12 = f32[2,2,8,2048]{3,2,1,0:T(8,128)} copy(f32[2,2,8,2048]{3,2,1,0:T(8,128)} %get-tuple-element.4) | data formatting | bytes 524288
  59.1 0.0 copy-done
  59.1 0.5 copy.13
Async XLA Ops:
  57.4 1.7 %copy-start = (f32[1,2]{1,0:T(1,128)S(1)}, f32[1,2]{1,0:T(1,128)}, u32[]{:S(2)}) copy-start(f32[1,2]{1,0:T(1,128)} %get-tuple-element.5) | copy-start | bytes 28

commit v3 on v2

v3 whole, which is shorter than its diff:
```python
import functools

import jax
import jax.numpy as jnp
from jax import lax
from jax.experimental import pallas as pl
from jax.experimental.pallas import tpu as pltpu
from jax.sharding import PartitionSpec as P

MESH = pl.DeviceIdType.MESH
SCALE = 0.2
F32 = jnp.float32


NX, NY, ZLO, ZHI, NC = 4, 8, 3, 4, 2


def remote(src, dst, send_sem, recv_sem, device):
    return pltpu.make_async_remote_copy(
        src_ref=src,
        dst_ref=dst,
        send_sem=send_sem,
        recv_sem=recv_sem,
        device_id=device,
        device_id_type=MESH,
    )


def kernel(
    tiles,
    layers,
    adjoint_in,
    source_in,
    viscosity_in,
    vertical_in,
    friction_in,
    mask_in,
    cells_in,
    owner_in,
    out,
    flux,
    adjoint,
    source,
    viscosity,
    vertical,
    friction,
    mask,
    cells,
    owner,
    halo,
    rims,
    rhs,
    gathered,
    solved,
    inverse,
    ratio,
    table,
    select,
    block_cells,
    cell_rows_out,
    cell_rows_in,
    gate_rows,
    picked,
    parts,
    load_sem,
    halo_send,
    halo_recv,
    rhs_send,
    rhs_recv,
    back_send,
    back_recv,
    own_send,
    own_recv,
    table_send,
    table_recv,
    rows_send,
    rows_recv,
    part_send,
    part_recv,
    self_sem,
    halo_ready,
    layer_ready,
    late_ready,
):
    tile = lax.axis_index("tile")
    layer = lax.axis_index("layer")
    nz = vertical.shape[0]
    per_layer = nz // layers
    width = rhs.shape[3]
    rows = rhs.shape[2]
    core, y, z_lo = tile % NC, (tile // NC) % NY, tile // (NC * NY)
    x, z_hi = layer % NX, layer // NX
    xy = y * NX + x
    zc = (z_hi * ZLO + z_lo) * NC + core
    n_xy, n_zc = NX * NY, ZHI * ZLO * NC

    def loop(low, high, fn):
        def one(i, carry):
            fn(i)
            return carry

        lax.fori_loop(low, high, one, 0)

    def at_layer(s):
        return {"tile": tile, "layer": layer ^ s}

    def at_xy(s):
        return {"tile": tile ^ ((s >> 2) << 1), "layer": layer ^ (s & (NX - 1))}

    def zc_parts(j):
        z = z_lo + (j >> 3)
        return z_hi ^ (j & 3), jnp.where(z >= ZLO, z - ZLO, z), core ^ ((j >> 2) & 1)

    def zc_index(j):
        high, low, c = zc_parts(j)
        return (high * ZLO + low) * NC + c

    def at_zc(j):
        _, low, c = zc_parts(j)
        return {"tile": low * (NY * NC) + (tile & (NY * NC - NC)) + c, "layer": layer ^ ((j & 3) << 2)}

    def rank_of(a):
        return jnp.where(a < NY // 2, a, NY + NY // 2 - 1 - a)

    def signal(sem, device):
        pl.semaphore_signal(sem, inc=1, device_id=device, device_id_type=MESH)

    def arrived(ref, sem):
        pltpu.make_async_copy(ref, ref, sem).wait()

    y_rank = rank_of(y)
    loads = []
    for i, (a, b) in enumerate(
        (
            (adjoint_in, adjoint),
            (source_in, source),
            (viscosity_in, viscosity),
            (vertical_in, vertical),
            (friction_in, friction),
            (mask_in, mask),
            (cells_in, cells),
            (owner_in, owner),
        )
    ):
        copy = pltpu.make_async_copy(a, b, load_sem.at[i])
        copy.start()
        loads.append(copy)

    barrier = pltpu.get_barrier_semaphore()
    has_up, has_down = tile > 0, tile < tiles - 1

    @pl.when(has_down)
    def _():
        signal(barrier, {"tile": tile + 1, "layer": layer})

    def greet_layer(s):
        @pl.when(layer ^ s > layer)
        def _():
            signal(barrier, at_layer(s))

    loop(1, layers, greet_layer)

    def greet_xy(s):
        @pl.when(rank_of(y ^ (s >> 2)) > y_rank)
        def _():
            signal(barrier, at_xy(s))

    loop(NX, n_xy, greet_xy)

    def greet_zc(j):
        @pl.when(zc_index(j) > zc)
        def _():
            signal(barrier, at_zc(j))

    loop(ZHI, n_zc, greet_zc)

    lower = layer + y_rank * NX + zc - z_hi + has_up.astype(jnp.int32)

    @pl.when(lower > 0)
    def _():
        pl.semaphore_wait(barrier, lower)

    @pl.when(has_up)
    def _():
        signal(halo_ready, {"tile": tile - 1, "layer": layer})

    def answer_layer(s):
        @pl.when(layer ^ s < layer)
        def _():
            signal(layer_ready.at[s], at_layer(s))

    loop(layers // 2, layers, answer_layer)
    loop(1, layers // 2, answer_layer)

    to_down = remote(
        rims.at[1],
        halo.at[0],
        halo_send.at[0],
        halo_recv.at[0],
        {"tile": tile + 1, "layer": layer},
    )
    to_up = remote(
        rims.at[0],
        halo.at[1],
        halo_send.at[1],
        halo_recv.at[1],
        {"tile": tile - 1, "layer": layer},
    )
    loads[0].wait()
    for side, row in enumerate((0, rows - 1)):
        for k in range(per_layer):
            for c in range(2):
                rims[side, 2 * k + c : 2 * k + c + 1] = adjoint[k, c, row : row + 1]

    @pl.when(has_up)
    def _():
        to_up.start()

    loads[1].wait()
    loads[2].wait()
    lane = lax.broadcasted_iota(jnp.int32, (1, width), 1)
    first_col, last_col = lane == 0, lane == width - 1
    sub = lax.broadcasted_iota(jnp.int32, (rows, 1), 0)

    def sideways(a):
        left = jnp.where(first_col, 0.0, pltpu.roll(a, 1, 1))
        right = jnp.where(last_col, 0.0, pltpu.roll(a, width - 1, 1))
        return left, right

    for k in range(per_layer):
        coef = SCALE * viscosity[k]
        value, diff, flat = [], [], []
        for c in range(2):
            a = adjoint[k, c]
            left, right = sideways(a)
            value.append(a)
            diff.append(0.25 * (right - left))
            flat.append(left + right - 4.0 * a)
        for c in range(2):
            above = jnp.where(sub == 0, 0.0, pltpu.roll(value[c] - diff[1 - c], 1, 0))
            below = jnp.where(sub == rows - 1, 0.0, pltpu.roll(value[c] + diff[1 - c], rows - 1, 0))
            rhs[k, c] = source[k, c] + coef * (flat[c] + (above + below))

    def rhs_copy(s):
        peer = layer ^ s
        return remote(
            rhs.at[:, :, :, pl.ds(pl.multiple_of(peer * 128, 128), 128)],
            gathered.at[pl.ds(layer * per_layer, per_layer)],
            rhs_send,
            rhs_recv,
            at_layer(s),
        )

    def own_copy(s):
        return remote(
            cell_rows_out.at[pl.ds(layer ^ s, 1)],
            cell_rows_in.at[pl.ds(layer, 1)],
            own_send,
            own_recv,
            at_layer(s),
        )

    def send_low(s):
        @pl.when(layer ^ s < layer)
        def _():
            rhs_copy(s).start()


    def answer_xy(s):
        @pl.when(rank_of(y ^ (s >> 2)) < y_rank)
        def _():
            signal(late_ready, at_xy(s))

    def answer_zc(j):
        @pl.when(zc_index(j) < zc)
        def _():
            signal(late_ready, at_zc(j))

    loop(NX, n_xy, answer_xy)
    loop(ZHI, n_zc, answer_zc)

    for c in loads[3:]:
        c.wait()
    count = cells.shape[1]
    gates = owner.shape[0] * 128
    owner_ids = tile * layers + lax.broadcasted_iota(jnp.int32, (layers, 128), 0)
    lane128 = lax.broadcasted_iota(jnp.int32, (layers, 128), 1)
    far = jnp.full((layers, 128), gates, jnp.int32)
    for j in range(owner.shape[0]):
        mine = owner[pl.ds(j, 1), :] == owner_ids
        far = jnp.minimum(far, jnp.where(mine, lane128 + j * 128, gates))
    first = jnp.min(far, axis=1, keepdims=True)
    for j in range(owner.shape[0]):
        mine = owner[pl.ds(j, 1), :] == owner_ids
        is_first = (lane128 + j * 128) == first
        select[0:layers, j * 128 : (j + 1) * 128] = jnp.where(mine & is_first, 1.0, 0.0)
        select[layers : 2 * layers, j * 128 : (j + 1) * 128] = jnp.where(
            mine & jnp.logical_not(is_first), 1.0, 0.0
        )
    select[:, gates:] = jnp.zeros((2 * layers, select.shape[1] - gates), F32)
    base = (layer * count) // 128
    shift = layer * count - base * 128
    block_cells[...] = jnp.zeros_like(block_cells)
    block_cells[:, 0:count] = cells[...].astype(F32)
    window = select[:, pl.ds(pl.multiple_of(base * 128, 128), 256)]
    window = pltpu.roll(window, lax.rem(256 - shift, 256), 1)[:, 0:128]
    chosen = lax.dot_general(
        window,
        block_cells[...],
        (((1,), (1,)), ((), ())),
        precision=lax.Precision.HIGHEST,
        preferred_element_type=F32,
    )
    cell_rows_out[...] = jnp.concatenate([chosen[0:layers], chosen[layers:]], axis=1)
    cell_rows_in[pl.ds(layer, 1)] = cell_rows_out[pl.ds(layer, 1)]

    active = mask[...].astype(F32)
    beneath = friction[...]
    link = jnp.zeros_like(beneath)
    ratio_prev = jnp.zeros_like(beneath)
    for k in range(nz):
        v = vertical[k]
        inv = 1.0 / (1.0 + beneath + v - link * ratio_prev)
        ratio_prev = v * inv
        inverse[k] = inv
        ratio[k] = ratio_prev
        beneath = v
        link = v

    @pl.when(has_down)
    def _():
        pl.semaphore_wait(halo_ready, 1)
        to_down.start()

    def beside(side, row, sign):
        for k in range(per_layer):
            factor = SCALE * viscosity[k, row : row + 1]
            for c in range(2):
                left, right = sideways(halo[side, 2 * k + 1 - c : 2 * k + 2 - c])
                term = halo[side, 2 * k + c : 2 * k + c + 1] + (sign * 0.25) * (right - left)
                rhs[k, c, row : row + 1] += factor * term

    @pl.when(has_up)
    def _():
        to_down.wait_recv()
        beside(0, 0, -1.0)

    @pl.when(has_down)
    def _():
        to_up.wait_recv()
        beside(1, rows - 1, 1.0)

    def both(fn):
        loop(layers // 2, layers, fn)
        loop(1, layers // 2, fn)

    loop(layers // 2, layers, send_low)
    loop(1, layers // 2, send_low)
    def send_high(p):
        s = layer ^ p
        pl.semaphore_wait(layer_ready.at[s], 1)
        rhs_copy(s).start()

    loop(layer + 1, layers, send_high)

    both(lambda s: own_copy(s).start())
    here = pl.ds(pl.multiple_of(layer * 128, 128), 128)
    for k in range(per_layer):
        for c in range(2):
            gathered[layer * per_layer + k, c] = rhs[k, c, :, here]

    arrived(cell_rows_in.at[pl.ds(0, layers - 1)], own_recv)
    gate_rows[pl.ds(zc, 1)] = jnp.sum(cell_rows_in[...], axis=0, keepdims=True)
    answers = (NY - 1 - y_rank) * NX + (n_zc - 1 - zc) - (ZHI - 1 - z_hi)

    @pl.when(answers > 0)
    def _():
        pl.semaphore_wait(late_ready, answers)

    def rows_copy(j):
        return remote(gate_rows.at[pl.ds(zc, 1)], gate_rows.at[pl.ds(zc, 1)], rows_send, rows_recv, at_zc(j))

    loop(1, n_zc, lambda j: rows_copy(j).start())

    some = pl.ds(0, (layers - 1) * per_layer)
    most = pl.ds(0, (layers - 1) * 128)
    arrived(gathered.at[some], rhs_recv)
    scaled = [jnp.zeros((rows, 128), F32)] * 2
    for k in range(nz):
        inv = inverse[k]
        for c in range(2):
            r = gathered[k, c]
            scaled[c] = (r + vertical[k - 1] * scaled[c]) * inv if k else r * inv
            solved[k, c] = scaled[c]
    upper = [jnp.zeros((rows, 128), F32)] * 2
    total = jnp.zeros((rows, 128), F32)
    for k in reversed(range(nz)):
        for c in range(2):
            upper[c] = solved[k, c] + ratio[k] * upper[c] if k < nz - 1 else solved[k, c]
            x_new = upper[c] * active
            solved[k, c] = x_new
            total = total + x_new
    table[xy] = total * (1.0 / nz)

    def table_copy(s):
        return remote(table.at[xy], table.at[xy], table_send, table_recv.at[s], at_xy(s))

    loop(n_xy // 2, n_xy, lambda s: table_copy(s).start())
    loop(1, n_xy // 2, lambda s: table_copy(s).start())

    def back_copy(s):
        return remote(
            solved.at[pl.ds((layer ^ s) * per_layer, per_layer)],
            out.at[:, :, :, here],
            back_send,
            back_recv,
            at_layer(s),
        )

    both(lambda s: back_copy(s).start())
    keep = pltpu.make_async_copy(solved.at[pl.ds(layer * per_layer, per_layer)], out.at[:, :, :, here], self_sem)
    keep.start()

    arrived(gate_rows.at[pl.ds(0, n_zc - 1)], rows_recv)
    groups = n_zc // 8
    where, lanes = [], []
    for v in range(groups):
        cell = gate_rows[v * 8 : (v + 1) * 8].astype(jnp.int32)
        row, col = cell // width, cell % width
        t, piece = row // rows, col // 128
        inside = (t % NC == core) & (t // (NC * NY) == z_lo) & (piece // NX == z_hi)
        spot = (((t // NC) % NY) * NX + piece % NX) * rows + row % rows
        where.append(jnp.where(inside, spot, -1))
        lanes.append(col % 128)

    def look(dy, found):
        found = list(found)
        for dx in range(NX):
            s = dy * NX + dx

            @pl.when(s > 0)
            def _():
                table_copy(s).wait_recv()

        for dx in range(NX):
            q = xy ^ (dy * NX + dx)
            for r in range(rows):
                line = jnp.broadcast_to(table[q, r : r + 1], (8, 128))
                for v in range(groups):
                    got = jnp.take_along_axis(line, lanes[v], axis=1, mode="promise_in_bounds")
                    found[v] = jnp.where(where[v] == q * rows + r, got, found[v])
        return tuple(found)

    found = tuple(jnp.zeros((8, 128), F32) for _ in range(groups))
    for low, high in ((0, NY // 2), (NY // 2 + 1, NY), (NY // 2, NY // 2 + 1)):
        found = lax.fori_loop(low, high, look, found)
    for v in range(groups):
        picked[v * 8 : (v + 1) * 8] = found[v]

    def part_copy(j):
        return remote(picked.at[pl.ds(zc_index(j), 1)], parts.at[pl.ds(zc, 1)], part_send, part_recv, at_zc(j))

    loop(1, n_zc, lambda j: part_copy(j).start())
    parts[pl.ds(zc, 1)] = picked[pl.ds(zc, 1)]
    arrived(out.at[:, :, :, most], back_recv)
    keep.wait()

    @pl.when(has_up)
    def _():
        to_up.wait_send()

    @pl.when(has_down)
    def _():
        to_down.wait_send()

    arrived(rhs.at[:, :, :, most], rhs_send)
    arrived(cell_rows_out.at[pl.ds(0, layers - 1)], own_send)
    arrived(gate_rows.at[pl.ds(0, n_zc - 1)], rows_send)
    arrived(table.at[pl.ds(0, n_xy - 1)], table_send)
    arrived(picked.at[pl.ds(0, n_zc - 1)], part_send)
    arrived(solved.at[some], back_send)
    arrived(parts.at[pl.ds(0, n_zc - 1)], part_recv)
    line = jnp.sum(parts[...], axis=0, keepdims=True)
    half = lax.broadcasted_iota(jnp.int32, (1, 128), 1) < 64
    slot0 = jnp.sum(jnp.where(half, line, 0.0), axis=1, keepdims=True)
    slot1 = jnp.sum(jnp.where(half, 0.0, line), axis=1, keepdims=True)
    flux[...] = jnp.where(lax.broadcasted_iota(jnp.int32, (1, 2), 1) == 0, slot0, slot1)


def solution(mesh):
    tiles, layers = mesh.shape["tile"], mesh.shape["layer"]
    n_xy, n_zc = NX * NY, ZHI * ZLO * NC
    assert tiles == ZLO * NY * NC and layers == ZHI * NX

    def local(adjoint, source, viscosity, vertical, friction, ice_mask, gate_cells, gate_owner):
        owner = gate_owner.reshape(-1, 128)
        gate_cells = gate_cells.T
        per_layer, _, rows, width = adjoint.shape
        nz = vertical.shape[0]
        vmem, dma = pltpu.VMEM, pltpu.SemaphoreType.DMA
        scratch = [
            vmem(a.shape, a.dtype)
            for a in (adjoint, source, viscosity, vertical, friction, ice_mask, gate_cells, owner)
        ]
        scratch += [
            vmem((2, 2 * per_layer, width), F32),
            vmem((2, 2 * per_layer, width), F32),
            vmem(adjoint.shape, F32),
            vmem((nz, 2, rows, 128), F32),
            vmem((nz, 2, rows, 128), F32),
            vmem((nz, rows, 128), F32),
            vmem((nz, rows, 128), F32),
            vmem((n_xy, rows, 128), F32),
            vmem((2 * layers, owner.size + 128), F32),
            vmem((gate_cells.shape[0], 128), F32),
            vmem((layers, 128), F32),
            vmem((layers, 128), F32),
            vmem((n_zc, 128), F32),
            vmem((n_zc, 128), F32),
            vmem((n_zc, 128), F32),
            dma((8,)),
        ]
        scratch += [dma((2,)), dma((2,))]
        scratch += [dma] * 6
        scratch += [dma, dma((n_xy,))]
        scratch += [dma] * 4
        plain = pltpu.SemaphoreType.REGULAR
        scratch += [dma, plain, plain((layers,)), plain]
        return pl.pallas_call(
            functools.partial(kernel, tiles, layers),
            out_shape=(
                jax.ShapeDtypeStruct(adjoint.shape, F32),
                jax.ShapeDtypeStruct((1, 2), F32),
            ),
            in_specs=[pl.BlockSpec(memory_space=pltpu.HBM)] * 8,
            out_specs=(
                pl.BlockSpec(memory_space=pl.ANY),
                pl.BlockSpec(memory_space=pltpu.VMEM),
            ),
            scratch_shapes=scratch,
            compiler_params=pltpu.CompilerParams(
                collective_id=0, has_side_effects=True, vmem_limit_bytes=55228 * 1024
            ),
            name="update",
        )(adjoint, source, viscosity, vertical, friction, ice_mask, gate_cells, owner)

    return jax.shard_map(
        local,
        mesh=mesh,
        in_specs=(
            P("layer", None, "tile", None),
            P("layer", None, "tile", None),
            P("layer", "tile", None),
            P(None, "tile", "layer"),
            P("tile", "layer"),
            P("tile", "layer"),
            P("layer", None),
            P(),
        ),
        out_specs=(P("layer", None, "tile", None), P(("tile", "layer"), None)),
        check_vma=False,
    )
```

time: 59.7 us -> 55.8 us (0.935)
  the two profiles are of different devices: /device:TPU:1 before, /device:TPU:25 now
where the time goes in v3:
time: 55.8 us; the launch traced here: 55.7 us
  Pallas kernels  52.8 us (95%)
  local copies, waits for them, and re-layouts  2.18 us (4%)
  between operations  0.64 us (1%)
    pallas_call x1, Pallas kernels, local(): pl.pallas_call(functools.partial(kernel, tiles, layers), out_shape=(jax.S...  52.8 us
    unnamed x2, local copies, waits for them, and re-layouts  2.18 us

profile of v3, /device:TPU:25, one launch (start us, length us, event | category | flops | bytes accessed | tf_op | source)
XLA Modules:
  0.0 55.7 jit_solution(9749270281638842125)
XLA Ops:
  0.6 52.8 %update.1 = (f32[2,2,8,2048]{3,2,1,0:T(8,128)}, f32[1,2]{1,0:T(1,128)S(1)}) custom-call(f32[2,2,8,2048]{3,2,1,0:T(8,128)} %adjoint_in.1, f32[2,2,8,2048]{3,2,1,0:T(8,128)} %source_in.1, f32[2,8,2048]{2,1,0:T(8,128)} %viscosity_in.1, f32[32,8,128]{2,1,0:T(8,128)} %vertical_in.1, f32[8,128]{1,0:T(8,128)} %friction_in.1, s32[8,128]{1,0:T(8,128)} %mask_in.1, ...), custom_call_target="tpu_custom_call" | custom-call | tf_op jit(solution)/shard_map/update/pallas_call | solution.py:529
  53.5 1.7 %copy.12 = f32[2,2,8,2048]{3,2,1,0:T(8,128)} copy(f32[2,2,8,2048]{3,2,1,0:T(8,128)} %get-tuple-element.4) | data formatting | bytes 524288
  55.1 0.5 copy.13

commit v4 on v3

--- a/solution.py
+++ b/solution.py
@@ -95,6 +95,11 @@
     n_xy, n_zc = NX * NY, ZHI * ZLO * NC
 
     def loop(low, high, fn):
+        if isinstance(low, int) and isinstance(high, int):
+            for i in range(low, high):
+                fn(i)
+            return
+
         def one(i, carry):
             fn(i)
             return carry
@@ -165,7 +170,6 @@
         def _():
             signal(barrier, at_xy(s))
 
-    loop(NX, n_xy, greet_xy)
 
     def greet_zc(j):
         @pl.when(zc_index(j) > zc)
@@ -173,6 +177,7 @@
             signal(barrier, at_zc(j))
 
     loop(ZHI, n_zc, greet_zc)
+    loop(NX, n_xy, greet_xy)
 
     lower = layer + y_rank * NX + zc - z_hi + has_up.astype(jnp.int32)
 
@@ -264,6 +269,7 @@
         @pl.when(layer ^ s < layer)
         def _():
             rhs_copy(s).start()
+            own_copy(s).start()
 
 
     def answer_xy(s):
@@ -360,10 +366,10 @@
         s = layer ^ p
         pl.semaphore_wait(layer_ready.at[s], 1)
         rhs_copy(s).start()
+        own_copy(s).start()
 
     loop(layer + 1, layers, send_high)
 
-    both(lambda s: own_copy(s).start())
     here = pl.ds(pl.multiple_of(layer * 128, 128), 128)
     for k in range(per_layer):
         for c in range(2):

time: 55.8 us -> 53.7 us (0.962)
  the two profiles are of different devices: /device:TPU:25 before, /device:TPU:49 now
where the time goes in v4:
time: 53.7 us; the launch traced here: 53.5 us
  Pallas kernels  50.7 us (94%)
  local copies, waits for them, and re-layouts  2.18 us (4%)
  between operations  0.64 us (1%)
    pallas_call x1, Pallas kernels, local(): pl.pallas_call(functools.partial(kernel, tiles, layers), out_shape=(jax.S...  50.7 us
    unnamed x2, local copies, waits for them, and re-layouts  2.18 us

profile of v4, /device:TPU:49, one launch (start us, length us, event | category | flops | bytes accessed | tf_op | source)
XLA Modules:
  0.0 53.5 jit_solution(624832824558785664)
XLA Ops:
  0.6 50.7 %update.1 = (f32[2,2,8,2048]{3,2,1,0:T(8,128)}, f32[1,2]{1,0:T(1,128)S(1)}) custom-call(f32[2,2,8,2048]{3,2,1,0:T(8,128)} %adjoint_in.1, f32[2,2,8,2048]{3,2,1,0:T(8,128)} %source_in.1, f32[2,8,2048]{2,1,0:T(8,128)} %viscosity_in.1, f32[32,8,128]{2,1,0:T(8,128)} %vertical_in.1, f32[8,128]{1,0:T(8,128)} %friction_in.1, s32[8,128]{1,0:T(8,128)} %mask_in.1, ...), custom_call_target="tpu_custom_call" | custom-call | tf_op jit(solution)/shard_map/update/pallas_call | solution.py:535
  51.3 1.7 %copy.12 = f32[2,2,8,2048]{3,2,1,0:T(8,128)} copy(f32[2,2,8,2048]{3,2,1,0:T(8,128)} %get-tuple-element.4) | data formatting | bytes 524288
  53.0 0.5 copy.13

commit v5 on v4

--- a/solution.py
+++ b/solution.py
@@ -412,7 +412,6 @@
         return remote(table.at[xy], table.at[xy], table_send, table_recv.at[s], at_xy(s))
 
     loop(n_xy // 2, n_xy, lambda s: table_copy(s).start())
-    loop(1, n_xy // 2, lambda s: table_copy(s).start())
 
     def back_copy(s):
         return remote(
@@ -424,6 +423,7 @@
         )
 
     both(lambda s: back_copy(s).start())
+    loop(1, n_xy // 2, lambda s: table_copy(s).start())
     keep = pltpu.make_async_copy(solved.at[pl.ds(layer * per_layer, per_layer)], out.at[:, :, :, here], self_sem)
     keep.start()
 

time: 53.7 us -> 53.7 us (level)
  the two profiles are of different devices: /device:TPU:49 before, /device:TPU:48 now
where the time goes in v5:
time: 53.7 us; the launch traced here: 53.5 us
  Pallas kernels  50.7 us (94%)
  local copies, waits for them, and re-layouts  2.18 us (4%)
  between operations  0.64 us (1%)
    pallas_call x1, Pallas kernels, local(): pl.pallas_call(functools.partial(kernel, tiles, layers), out_shape=(jax.S...  50.7 us
    unnamed x2, local copies, waits for them, and re-layouts  2.18 us

profile of v5, /device:TPU:48, one launch (start us, length us, event | category | flops | bytes accessed | tf_op | source)
XLA Modules:
  0.0 53.5 jit_solution(6124180127250656706)
XLA Ops:
  0.6 50.7 %update.1 = (f32[2,2,8,2048]{3,2,1,0:T(8,128)}, f32[1,2]{1,0:T(1,128)S(1)}) custom-call(f32[2,2,8,2048]{3,2,1,0:T(8,128)} %adjoint_in.1, f32[2,2,8,2048]{3,2,1,0:T(8,128)} %source_in.1, f32[2,8,2048]{2,1,0:T(8,128)} %viscosity_in.1, f32[32,8,128]{2,1,0:T(8,128)} %vertical_in.1, f32[8,128]{1,0:T(8,128)} %friction_in.1, s32[8,128]{1,0:T(8,128)} %mask_in.1, ...), custom_call_target="tpu_custom_call" | custom-call | tf_op jit(solution)/shard_map/update/pallas_call | solution.py:535
  51.4 1.7 %copy.12 = f32[2,2,8,2048]{3,2,1,0:T(8,128)} copy(f32[2,2,8,2048]{3,2,1,0:T(8,128)} %get-tuple-element.4) | data formatting | bytes 524288
  53.0 0.5 copy.13
